TPU v7x, 32 devices: a whole 2x2x4 slice. The times are simulated.
32 devices in a mesh: lat: 8 (over z, x), lon: 4 (over y, core).
Axes of the slice: x: 2, y: 2, z: 4, core: 2. Of those that a mesh axis runs over, the one named last changes fastest.
Arguments:
- thickness: float32 [2, 1024, 8192], P(None, 'lat', 'lon'), may hold values from 0.5 to 1.5
- winds: float32 [2, 2, 1024, 8192], P(None, None, 'lat', 'lon'), may hold values from -3 to 3
- terrain: float32 [1024, 8192], P('lat', 'lon'), may hold values from -1.5 to 1.5
- cutoffs: int32 [342], replicated, may hold values from 1 to 4096, as said below
Outputs:
- new_thickness: float32 [2, 1024, 8192], P(None, 'lat', 'lon')
- new_winds: float32 [2, 2, 1024, 8192], P(None, None, 'lat', 'lon')
Inputs may be any that keep to these rules, and one draw needn't show every extreme that they name: cutoffs[p] is the count of the lowest zonal wavenumbers kept on cap row p (the 171 southernmost rows from south to north, then the 171 northernmost).
All inputs are finite; a program needn't handle non-finite values.
Results may differ from a plain program's by a relative error of at most 0.0003.
Values sent between devices are 32-bit elements; how exact they have to be, the bound alone decides.
A program may use at most 128 MiB of HBM per device.

v0:
```python
import math

import jax
import jax.numpy as jnp
from jax import lax
from jax.sharding import PartitionSpec as P

GRAVITY = 1.0
DENSITY_RATIO = 0.9
CORIOLIS = 1.0


def padded_2(cells, sides, width, closed):
    for axis, dim in sides:
        count = lax.axis_size(axis)
        ends = count if closed else count - 1
        head = lax.slice_in_dim(cells, 0, width, axis=dim)
        tail = lax.slice_in_dim(cells, cells.shape[dim] - width, cells.shape[dim], axis=dim)
        cells = jnp.concatenate(
            [
                lax.ppermute(tail, axis, [(i, (i + 1) % count) for i in range(ends)]),
                cells,
                lax.ppermute(head, axis, [((i + 1) % count, i) for i in range(ends)]),
            ],
            axis=dim,
        )
    return cells


def stencil_tendency(padded, row_start, total_rows, circle):
    row_count = padded.shape[1] - 2
    thickness = padded[0:2]
    zonal_wind = padded[2:4]
    ground = padded[6]
    row_ids = row_start - 1 + jnp.arange(row_count + 2, dtype=jnp.int32)
    spacing = math.pi / total_rows
    centre_lat = -0.5 * math.pi + (row_ids.astype(jnp.float32) + 0.5) * spacing
    face_lat = -0.5 * math.pi + (row_ids.astype(jnp.float32) + 1.0) * spacing
    face_live = jnp.where((row_ids >= 0) & (row_ids < total_rows - 1), 1.0, 0.0).astype(jnp.float32)
    centre_cos = jnp.cos(centre_lat)
    face_cos = jnp.cos(face_lat) * face_live
    face_inverse = face_live / (face_cos + (1.0 - face_live))
    merid_step = circle / (2.0 * total_rows)
    merid_wind = padded[4:6] * face_live[None, :, None]
    inner_cosine = centre_cos[1:-1][None, :, None]
    flux_east = 0.5 * (thickness[:, :, :-1] + thickness[:, :, 1:]) * zonal_wind[:, :, :-1]
    flux_north = (
        0.5
        * (thickness[:, :-1, :] + thickness[:, 1:, :])
        * merid_wind[:, :-1, :]
        * face_cos[:-1][None, :, None]
    )
    converge = (
        flux_east[:, 1:-1, 1:]
        - flux_east[:, 1:-1, :-1]
        + (flux_north[:, 1:, 1:-1] - flux_north[:, :-1, 1:-1]) / merid_step
    )
    thick_tend = -converge / inner_cosine
    kinetic = 0.25 * (
        zonal_wind[:, 1:, 1:] ** 2
        + zonal_wind[:, 1:, :-1] ** 2
        + merid_wind[:, 1:, 1:] ** 2
        + merid_wind[:, :-1, 1:] ** 2
    )
    upper_layer = thickness[0, 1:, 1:]
    lower_layer = thickness[1, 1:, 1:]
    surface = ground[1:, 1:]
    potential = jnp.stack(
        [
            GRAVITY * (upper_layer + lower_layer + surface),
            GRAVITY * (DENSITY_RATIO * upper_layer + lower_layer + surface),
        ]
    )
    energy = kinetic + potential
    merid_diff = merid_wind[:, :-1, 1:] - merid_wind[:, :-1, :-1]
    zonal_diff = (
        zonal_wind[:, 1:, :-1] * centre_cos[1:][None, :, None]
        - zonal_wind[:, :-1, :-1] * centre_cos[:-1][None, :, None]
    )
    absolute = (
        CORIOLIS * jnp.sin(face_lat[:-1])[None, :, None]
        + (merid_diff - zonal_diff / merid_step) * face_inverse[:-1][None, :, None]
    )
    merid_mean = 0.25 * (
        merid_wind[:, 1:-1, 1:-1]
        + merid_wind[:, 1:-1, 2:]
        + merid_wind[:, :-2, 1:-1]
        + merid_wind[:, :-2, 2:]
    )
    zonal_mean = 0.25 * (
        zonal_wind[:, 1:-1, 1:-1]
        + zonal_wind[:, 1:-1, :-2]
        + zonal_wind[:, 2:, 1:-1]
        + zonal_wind[:, 2:, :-2]
    )
    centre_energy = energy[:, :-1, :-1]
    east_energy = energy[:, :-1, 1:]
    north_energy = energy[:, 1:, :-1]
    zonal_tend = (
        0.5 * (absolute[:, 1:, 1:] + absolute[:, :-1, 1:]) * merid_mean
        - (east_energy - centre_energy) / inner_cosine
    )
    merid_tend = (
        -0.5 * (absolute[:, 1:, 1:] + absolute[:, 1:, :-1]) * zonal_mean
        - (north_energy - centre_energy) / merid_step
    ) * face_live[1:-1][None, :, None]
    return jnp.concatenate([thick_tend, zonal_tend, merid_tend], axis=0)


def spectral_filter(flat, keep_count):
    circle = flat.shape[1]
    second = 128
    first = circle // second
    index_first = jnp.arange(first, dtype=jnp.int32)
    index_second = jnp.arange(second, dtype=jnp.int32)
    angle_first = (
        2.0
        * math.pi
        / first
        * (index_first[:, None] * index_first[None, :] % first).astype(jnp.float32)
    )
    angle_second = (
        2.0
        * math.pi
        / second
        * (index_second[:, None] * index_second[None, :] % second).astype(jnp.float32)
    )
    angle_twist = (
        2.0
        * math.pi
        / circle
        * (index_first[:, None] * index_second[None, :] % circle).astype(jnp.float32)
    )
    cos_first, sin_first = (jnp.cos(angle_first), jnp.sin(angle_first))
    cos_second, sin_second = (jnp.cos(angle_second), jnp.sin(angle_second))
    cos_twist, sin_twist = (jnp.cos(angle_twist), jnp.sin(angle_twist))
    highest = lax.Precision.HIGHEST
    grid = flat.reshape(flat.shape[0], first, second)
    part_real = jnp.einsum("mab,ak->mkb", grid, cos_first, precision=highest)
    part_imag = -jnp.einsum("mab,ak->mkb", grid, sin_first, precision=highest)
    twist_real = part_real * cos_twist + part_imag * sin_twist
    twist_imag = part_imag * cos_twist - part_real * sin_twist
    spec_real = jnp.einsum("mkb,bl->mkl", twist_real, cos_second, precision=highest) + jnp.einsum(
        "mkb,bl->mkl", twist_imag, sin_second, precision=highest
    )
    spec_imag = jnp.einsum("mkb,bl->mkl", twist_imag, cos_second, precision=highest) - jnp.einsum(
        "mkb,bl->mkl", twist_real, sin_second, precision=highest
    )
    wavenumber = index_first[:, None] + first * index_second[None, :]
    folded = jnp.minimum(wavenumber, circle - wavenumber)
    keep = folded[None] < keep_count[:, None, None]
    spec_real = jnp.where(keep, spec_real, 0.0)
    spec_imag = jnp.where(keep, spec_imag, 0.0)
    back_real = jnp.einsum("mkl,lb->mkb", spec_real, cos_second, precision=highest) - jnp.einsum(
        "mkl,lb->mkb", spec_imag, sin_second, precision=highest
    )
    back_imag = jnp.einsum("mkl,lb->mkb", spec_real, sin_second, precision=highest) + jnp.einsum(
        "mkl,lb->mkb", spec_imag, cos_second, precision=highest
    )
    turn_real = back_real * cos_twist - back_imag * sin_twist
    turn_imag = back_real * sin_twist + back_imag * cos_twist
    signal = jnp.einsum("mkb,ka->mab", turn_real, cos_first, precision=highest) - jnp.einsum(
        "mkb,ka->mab", turn_imag, sin_first, precision=highest
    )
    return (signal / circle).reshape(flat.shape)


def filter_rows(circles, global_rows, cutoffs, total_rows, polar):
    channels = circles.shape[0]
    circle = circles.shape[-1]
    row_list = global_rows.reshape(-1)
    is_polar = (row_list < polar) | (row_list >= total_rows - polar)
    position = jnp.where(row_list < polar, row_list, row_list - (total_rows - 2 * polar))
    table_ids = jnp.arange(2 * polar, dtype=jnp.int32)
    keep_count = jnp.sum(
        jnp.where(position[:, None] == table_ids[None, :], cutoffs[None, :], 0),
        axis=1,
        dtype=jnp.int32,
    )
    flat = circles.reshape(channels * row_list.shape[0], circle)
    counts_all = jnp.tile(keep_count, channels)
    polar_all = jnp.tile(is_polar, channels)
    filtered = spectral_filter(flat, counts_all)
    return jnp.where(polar_all[:, None], filtered, flat).reshape(circles.shape)


def cap_filter(tendency, cutoffs, row_count, col_count, total_rows, polar):
    channels = tendency.shape[0]
    lat_count = lax.axis_size("lat")
    lon_count = lax.axis_size("lon")
    circle = col_count * lon_count
    device_count = lat_count * lon_count
    groups = row_count // device_count
    device_rank = lax.axis_index("lat") * lon_count + lax.axis_index("lon")
    outgoing = tendency.reshape(channels, groups, device_count, col_count)
    incoming = lax.all_to_all(outgoing, ("lat", "lon"), split_axis=2, concat_axis=2, tiled=True)
    circles = incoming.reshape(channels, groups, lat_count, circle)
    band_ids = jnp.arange(lat_count, dtype=jnp.int32)
    group_ids = jnp.arange(groups, dtype=jnp.int32)
    global_rows = band_ids[None, :] * row_count + group_ids[:, None] * device_count + device_rank
    cap_bands = min(lat_count, (polar + row_count - 1) // row_count)
    southern = filter_rows(
        circles[:, :, :cap_bands], global_rows[:, :cap_bands], cutoffs, total_rows, polar
    )
    northern = filter_rows(
        circles[:, :, lat_count - cap_bands :],
        global_rows[:, lat_count - cap_bands :],
        cutoffs,
        total_rows,
        polar,
    )
    filtered = jnp.concatenate(
        [southern, circles[:, :, cap_bands : lat_count - cap_bands], northern], axis=2
    )
    returning = lax.all_to_all(
        filtered.reshape(channels, groups, device_count, col_count),
        ("lat", "lon"),
        split_axis=2,
        concat_axis=2,
        tiled=True,
    )
    return returning.reshape(channels, row_count, col_count)


def body(thickness, winds, terrain, cutoffs):
    row_count = thickness.shape[1]
    col_count = thickness.shape[2]
    total_rows = row_count * lax.axis_size("lat")
    circle = col_count * lax.axis_size("lon")
    polar = (total_rows + 2) // 6
    row_start = lax.axis_index("lat") * row_count
    global_rows = row_start + jnp.arange(row_count, dtype=jnp.int32)
    live = jnp.where(global_rows < total_rows - 1, 1.0, 0.0).astype(jnp.float32)
    current = jnp.concatenate([thickness, winds[0], winds[1] * live[None, :, None]], axis=0)
    step_size = 0.1 * min(1.0, circle / (2.0 * total_rows))
    anchor = current
    for fraction in (1.0 / 3.0, 0.5, 1.0):
        stacked = jnp.concatenate([current, terrain[None]], axis=0)
        lat_rims = padded_2(stacked, (("lat", 1),), 1, False)
        padded = padded_2(lat_rims, (("lon", 2),), 1, True)
        tendency = stencil_tendency(padded, row_start, total_rows, circle)
        tendency = cap_filter(tendency, cutoffs, row_count, col_count, total_rows, polar)
        current = anchor + fraction * step_size * tendency
    return (current[0:2], current[2:6].reshape(2, 2, row_count, col_count))


def solution(mesh):
    in_specs = (P(None, "lat", "lon"), P(None, None, "lat", "lon"), P("lat", "lon"), P())
    out_specs = (P(None, "lat", "lon"), P(None, None, "lat", "lon"))
    return jax.shard_map(body, mesh=mesh, in_specs=in_specs, out_specs=out_specs, check_vma=False)
```

profile of v0, /device:TPU:0, one launch (start us, length us, event | category | flops | bytes accessed | tf_op | source)
XLA Modules:
  0.0 1548.2 jit_solution(1507317855434332305)
XLA Ops:
  10.1 4.8 collective-permute-start
  28.2 9.5 collective-permute-done.3
  41.0 10.8 concatenate.105
  56.1 18.7 %fusion.11 = (f32[7,130,2049]{2,1,0:T(8,128)}, f32[7,130,2049]{2,1,0:T(8,128)}) fusion(f32[1,128,2048]{2,1,0:T(8,128)S(1)} %bitcast.369, f32[7,1,2048]{2,1,0:T(1,128)S(1)} %collective-permute-done.1, f32[2,128,2048]{2,1,0:T(8,128)S(1)} %copy-done.3, f32[2,128,2048]{2,1,0:T(8,128)S(1)} %slice_bitcast_fusion, f32[2,128,2048]{2,1,0:T(8,128)S(1)} %copy-done.9, ...), kind=kLoop, calls=%fused_computation.22 | loop fusion | flops 22375080 | bytes 22378720 | tf_op jit(solution)/shard_map/concatenate | solution.py:19
  78.6 5.0 slice_multiply_fusion.17
  85.4 6.1 fusion.59
  91.5 10.0 fusion.116
  108.5 6.7 copy.18
  115.2 5.0 all-to-all-start
  121.2 139.0 %all-to-all-done = f32[6,4,32,2048]{3,1,0,2:T(4,128)} async-done(((f32[6,4,32,2048]{3,1,0,2:T(4,128)}), f32[6,4,32,2048]{3,1,0,2:T(4,128)}, u32[]{:S(2)}, u32[]{:S(2)}) %all-to-all-start) | async-done | bytes 6291488 | tf_op jit(solution)/shard_map/all_to_all | solution.py:196
  260.2 9.1 copy.19
  269.3 8.1 reshape.276
  277.3 5.5 slice.710
  354.1 6.7 broadcast_select_fusion.5
  364.5 7.9 reshape.280
  372.4 6.8 copy.20
  379.2 144.0 %all_to_all.30 = f32[6,4,32,2048]{3,1,0,2:T(4,128)S(1)} all-to-all(f32[6,4,32,2048]{3,1,0,2:T(4,128)S(1)} %copy.20), channel_id=1, replica_groups=mesh['lat'=8,'lon'=4] {'lat','lon'}, dimensions={2} | all-to-all | bytes 12582912 | tf_op jit(solution)/shard_map/all_to_all | solution.py:215
  544.9 10.0 collective-permute-done.7
  557.9 11.0 concatenate.113
  573.3 4.5 fusion.47
  577.8 15.6 %fusion.14 = (f32[7,130,2049]{2,1,0:T(8,128)S(1)}, f32[7,130,2049]{2,1,0:T(8,128)S(1)}) fusion(f32[1,128,2048]{2,1,0:T(8,128)S(1)} %bitcast.373, f32[7,1,2048]{2,1,0:T(1,128)S(1)} %collective-permute-done.5, f32[6,128,2048]{2,1,0:T(8,128)S(1)} %bitcast.366, f32[7,1,2048]{2,1,0:T(1,128)S(1)} %collective-permute-done.4, ...), kind=kLoop, calls=%fused_computation.25 | loop fusion | flops 14916720 | bytes 22378720 | tf_op jit(solution)/shard_map/concatenate | solution.py:19
  593.4 4.7 add_bitcast_fusion.3
  600.5 6.5 fusion.46
  607.0 13.3 fusion.105
  620.3 5.3 fusion.76
  632.3 141.1 %all_to_all.31 = f32[6,4,32,2048]{3,1,0,2:T(4,128)S(1)} all-to-all(f32[6,4,32,2048]{3,1,0,2:T(4,128)S(1)} %copy.22), channel_id=1, replica_groups=mesh['lat'=8,'lon'=4] {'lat','lon'}, dimensions={2} | all-to-all | bytes 12582912 | tf_op jit(solution)/shard_map/all_to_all | solution.py:196
  773.3 6.3 copy.23
  779.6 8.1 reshape.282
  787.7 5.5 slice.751
  864.4 6.7 broadcast_select_fusion.4
  874.8 7.9 reshape.285
  882.7 6.8 copy.24
  889.6 142.2 %all_to_all.32 = f32[6,4,32,2048]{3,1,0,2:T(4,128)S(1)} all-to-all(f32[6,4,32,2048]{3,1,0,2:T(4,128)S(1)} %copy.24), channel_id=1, replica_groups=mesh['lat'=8,'lon'=4] {'lat','lon'}, dimensions={2} | all-to-all | bytes 12582912 | tf_op jit(solution)/shard_map/all_to_all | solution.py:215
  1052.0 10.0 collective-permute-done.11
  1065.1 11.0 concatenate.121
  1084.9 15.6 %fusion.17 = (f32[7,130,2049]{2,1,0:T(8,128)S(1)}, f32[7,130,2049]{2,1,0:T(8,128)S(1)}) fusion(f32[1,128,2048]{2,1,0:T(8,128)S(1)} %bitcast.376, f32[7,1,2048]{2,1,0:T(1,128)S(1)} %collective-permute-done.9, f32[6,128,2048]{2,1,0:T(8,128)S(1)} %bitcast.364, f32[7,1,2048]{2,1,0:T(1,128)S(1)} %collective-permute-done.8, ...), kind=kLoop, calls=%fused_computation.28 | loop fusion | flops 14916720 | bytes 22378720 | tf_op jit(solution)/shard_map/concatenate | solution.py:19
  1100.5 4.7 add_bitcast_fusion.1
  1107.6 6.5 fusion.33
  1114.1 13.3 fusion.94
  1127.4 5.3 fusion.83
  1139.4 141.1 %all_to_all.33 = f32[6,4,32,2048]{3,1,0,2:T(4,128)S(1)} all-to-all(f32[6,4,32,2048]{3,1,0,2:T(4,128)S(1)} %copy.26), channel_id=1, replica_groups=mesh['lat'=8,'lon'=4] {'lat','lon'}, dimensions={2} | all-to-all | bytes 12582912 | tf_op jit(solution)/shard_map/all_to_all | solution.py:196
  1280.5 6.3 copy.27
  1286.8 8.1 reshape.287
  1294.9 5.5 slice.792
  1371.6 6.7 broadcast_select_fusion.3
  1382.0 7.7 reshape.290
  1389.7 6.8 copy.28
  1396.5 142.2 %all_to_all.34 = f32[6,4,32,2048]{3,1,0,2:T(4,128)S(1)} all-to-all(f32[6,4,32,2048]{3,1,0,2:T(4,128)S(1)} %copy.28), channel_id=1, replica_groups=mesh['lat'=8,'lon'=4] {'lat','lon'}, dimensions={2} | all-to-all | bytes 12582912 | tf_op jit(solution)/shard_map/all_to_all | solution.py:215
  (292 shorter events, 356.4 us)
Async XLA Ops:
  3.8 6.2 copy-start.2
  10.1 6.7 collective-permute-start
  14.9 6.1 collective-permute-start.1
  27.3 10.4 collective-permute-start.3
  27.4 13.6 collective-permute-start.2
  74.8 8.7 slice-start.4
  78.5 5.0 slice-start.5
  91.5 10.0 copy-start.17
  115.2 5.3 copy-start.52
  115.2 145.0 %all-to-all-start = ((f32[6,4,32,2048]{3,1,0,2:T(4,128)}), f32[6,4,32,2048]{3,1,0,2:T(4,128)}, u32[]{:S(2)}, u32[]{:S(2)}) async-start(f32[6,4,32,2048]{3,1,0,2:T(4,128)} %copy.18), calls=%async_computation | async-start | bytes 12582912 | tf_op jit(solution)/shard_map/all_to_all | solution.py:196
  277.3 5.5 copy-start.21
  289.5 4.3 copy-start.34
  338.9 4.2 copy-start.49
  354.1 6.7 copy-start.41
  523.2 4.1 copy-start.10
  528.8 11.0 copy-start.1
  530.3 5.2 collective-permute-start.4
  533.6 6.1 collective-permute-start.5
  544.3 10.6 collective-permute-start.7
  544.4 13.6 collective-permute-start.6
  571.3 6.5 slice-start.2
  573.3 4.5 slice-start.3
  593.4 7.1 copy-start.15
  593.4 7.1 copy-start.33
  607.0 13.3 copy-start.16
  607.0 13.3 copy-start.19
  620.2 5.3 copy-start.44
  787.7 5.5 copy-start.22
  799.9 4.3 copy-start.36
  849.2 4.2 copy-start.50
  864.4 6.7 copy-start.42
  1031.7 4.1 copy-start.11
  1037.3 9.6 copy-start
  1037.4 5.2 collective-permute-start.8
  1040.8 6.1 collective-permute-start.9
  1051.4 10.6 collective-permute-start.11
  1051.5 13.6 collective-permute-start.10
  1078.4 6.5 slice-start
  1080.5 4.5 slice-start.1
  1100.5 7.1 copy-start.13
  1100.5 7.1 copy-start.32
  1114.1 13.3 copy-start.14
  1114.1 13.3 copy-start.18
  1127.4 5.3 copy-start.43
  1294.8 5.5 copy-start.20
  1307.1 4.3 copy-start.38
  1356.4 4.2 copy-start.46
  1371.6 6.7 copy-start.40
  (24 other events, 62.9 us)
where the time goes:
time: 1550 us
  blocking collectives  710 us (46%)
  local copies, waits for them, and re-layouts  230 us (15%)
  other arithmetic  228 us (15%)
  waiting for transfers between devices  192 us (12%)
  matrix products  163 us (11%)
  starting transfers between devices  22.2 us (1%)
    all_to_all x3, blocking collectives, cap_filter(): lax.all_to_all(filtered.reshape(channels, groups, device_count, col_count...  428 us
    all_to_all x2, blocking collectives, cap_filter(): lax.all_to_all(outgoing, ('lat', 'lon'), split_axis=2, concat_axis=2, til...  282 us
    all_to_all x1, waiting for transfers between devices, cap_filter(): lax.all_to_all(outgoing, ('lat', 'lon'), split_axis=2, concat_axis=2, til...  139 us
    concatenate x6, other arithmetic, padded_2(): jnp.concatenate([lax.ppermute(tail, axis, [(i, (i + 1) % count) for i in...  55.4 us
    reshape x6, local copies, waits for them, and re-layouts, cap_filter(): filtered.reshape(channels, groups, device_count, col_count)  44 us
    ppermute x6, waiting for transfers between devices, padded_2(): lax.ppermute(head, axis, [((i + 1) % count, i) for i in range(ends)])  42.3 us
    div x3, other arithmetic, stencil_tendency(): thick_tend = -converge / inner_cosine  36.5 us
    concatenate x3, local copies, waits for them, and re-layouts, padded_2(): jnp.concatenate([lax.ppermute(tail, axis, [(i, (i + 1) % count) for i in...  32.7 us
  transfers between devices with their start and end apart: 13, of which 13 were waited for; matrix products, arithmetic and copies ran while one was open for 0% of the time, Pallas kernels for 0%

commit v1 on v0

v1 whole, which is shorter than its diff:
```python
import functools
import math

import jax
import jax.numpy as jnp
import numpy as np
from jax import lax
from jax.experimental import pallas as pl
from jax.experimental.pallas import tpu as pltpu
from jax.sharding import PartitionSpec as P

GRAVITY = 1.0
DENSITY_RATIO = 0.9
CORIOLIS = 1.0
LANES = 128
TILE = 8
MESH = pl.DeviceIdType.MESH
LIMIT = 56 * 1024 * 1024


def stencil_kernel(state_ref, rows_ref, cols_ref, ground_ref, coef_ref, out_ref, pad, sems):
    row_count, col_count = state_ref.shape[1:]
    window = 512
    wide = window + 2 * LANES
    merid_inverse = out_merid_inverse(col_count, row_count)
    inner_rows, inner_cols = pl.ds(TILE, row_count), pl.ds(LANES, col_count)
    copies = [
        (state_ref, pad.at[0:6, inner_rows, inner_cols]),
        (ground_ref, pad.at[6, inner_rows, inner_cols]),
        (rows_ref.at[:, 0:TILE], pad.at[:, 0:TILE, inner_cols]),
        (rows_ref.at[:, TILE : 2 * TILE], pad.at[:, pl.ds(TILE + row_count, TILE), inner_cols]),
        (cols_ref.at[:, :, 0:LANES], pad.at[:, :, 0:LANES]),
        (cols_ref.at[:, :, LANES : 2 * LANES], pad.at[:, :, pl.ds(LANES + col_count, LANES)]),
    ]
    started = [pltpu.make_async_copy(a, b, sems.at[i]) for i, (a, b) in enumerate(copies)]
    for copy in started:
        copy.start()
    for copy in started:
        copy.wait()

    def east(x):
        return pltpu.roll(x, wide - 1, 1)

    def west(x):
        return pltpu.roll(x, 1, 1)

    def triple(x):
        return x[TILE - 1 : 2 * TILE - 1], x[TILE : 2 * TILE], x[TILE + 1 : 2 * TILE + 1]

    def one(step, _):
        tile = step // (col_count // window)
        part = step % (col_count // window)
        rows = pl.ds(pl.multiple_of(tile * TILE, TILE), 3 * TILE)
        cols = pl.ds(pl.multiple_of(part * window, window), wide)

        def field(k):
            return triple(pad[k, rows, cols])

        def coef(k):
            return tuple(jnp.tile(x, (1, wide // LANES)) for x in triple(coef_ref[k, rows, :]))

        cm, co, cp = coef(0)
        inv = coef(1)[1]
        em, eo, _ = coef(2)
        sm, so, _ = coef(3)
        fm, fo, _ = coef(4)
        live = coef(5)[1]
        h0 = field(0)
        h1 = field(1)
        ground = field(6)
        out_rows = pl.ds(pl.multiple_of(tile * TILE, TILE), TILE)
        out_cols = pl.ds(pl.multiple_of(part * window, window), window)
        for layer in range(2):
            hm, ho, hp = h0 if layer == 0 else h1
            um, uo, up = field(2 + layer)
            vm, vo, vp = field(4 + layer)
            ratio = 1.0 if layer == 0 else DENSITY_RATIO
            flux = 0.5 * (ho + east(ho)) * uo
            north = 0.5 * (ho + hp) * vo * eo
            south = 0.5 * (hm + ho) * vm * em
            thick = -((flux - west(flux)) + (north - south) * merid_inverse) * inv
            squares = uo * uo
            energy = 0.25 * (squares + west(squares) + vo * vo + vm * vm) + (
                ratio * h0[1] + h1[1] + ground[1]
            )
            squares = up * up
            energy_north = 0.25 * (squares + west(squares) + vp * vp + vo * vo) + (
                ratio * h0[2] + h1[2] + ground[2]
            )
            curl_o = so + ((east(vo) - vo) - (up * cp - uo * co) * merid_inverse) * fo
            curl_m = sm + ((east(vm) - vm) - (uo * co - um * cm) * merid_inverse) * fm
            merid_sum = vo + vm
            zonal_sum = uo + up
            zonal = 0.125 * (curl_o + curl_m) * (merid_sum + east(merid_sum)) - (
                east(energy) - energy
            ) * inv
            merid = (
                -0.125 * (curl_o + west(curl_o)) * (zonal_sum + west(zonal_sum))
                - (energy_north - energy) * merid_inverse
            ) * live
            inside = slice(LANES, LANES + window)
            out_ref[layer, out_rows, out_cols] = thick[:, inside]
            out_ref[2 + layer, out_rows, out_cols] = zonal[:, inside]
            out_ref[4 + layer, out_rows, out_cols] = merid[:, inside]
        return 0

    lax.fori_loop(0, (row_count // TILE) * (col_count // window), one, 0)


def out_merid_inverse(col_count, row_count):
    circle = col_count * lax.axis_size("lon")
    total = row_count * lax.axis_size("lat")
    return 2.0 * total / circle


def stencil(state, rows, cols, ground, coefs):
    row_count, col_count = state.shape[1:]
    return pl.pallas_call(
        stencil_kernel,
        out_shape=jax.ShapeDtypeStruct(state.shape, jnp.float32),
        in_specs=[pl.BlockSpec(memory_space=pl.ANY)] * 4 + [pl.BlockSpec(memory_space=pltpu.VMEM)],
        out_specs=pl.BlockSpec(memory_space=pltpu.VMEM),
        scratch_shapes=[
            pltpu.VMEM((7, row_count + 2 * TILE, col_count + 2 * LANES), jnp.float32),
            pltpu.SemaphoreType.DMA((6,)),
        ],
        compiler_params=pltpu.CompilerParams(vmem_limit_bytes=LIMIT),
        name="stencil",
    )(state, rows, cols, ground, coefs)


def times(z, w):
    re, im = z
    wr, wi = w.real, w.imag
    if abs(wr) < 1e-12:
        return (None if im is None else im * (-wi), re * wi)
    if abs(wi) < 1e-12:
        return (re * wr, None if im is None else im * wr)
    if im is None:
        return (re * wr, re * wi)
    return (re * wr - im * wi, re * wi + im * wr)


def plus(a, b):
    return b if a is None else a if b is None else a + b


def minus(a, b):
    if b is None:
        return a
    return -b if a is None else a - b


def forward_real(x):
    n = len(x)
    if n == 2:
        return [(x[0] + x[1], None), (x[0] - x[1], None)]
    even, odd = forward_real(x[0::2]), forward_real(x[1::2])
    out = [None] * (n // 2 + 1)
    for k in range(n // 4 + 1):
        er, ei = even[k]
        tr, ti = (odd[k][0], odd[k][1]) if k == 0 else times(odd[k], np.exp(-2j * np.pi * k / n))
        out[k] = (plus(er, tr), plus(ei, ti))
        if k < n // 4:
            low = minus(ei, ti)
            out[n // 2 - k] = (minus(er, tr), None if low is None else -low)
    return out


def inverse_real(z):
    n = 2 * (len(z) - 1)
    if n == 2:
        return [z[0][0] + z[1][0], z[0][0] - z[1][0]]
    even, odd = [], []
    for k in range(n // 4 + 1):
        if k == n // 4:
            re, im = z[k]
            even.append((re + re, None))
            odd.append((-(im + im), None))
            continue
        ar, ai = z[k]
        br, bi = z[n // 2 - k]
        if k == 0:
            even.append((ar + br, None))
            odd.append((ar - br, None))
            continue
        even.append((plus(ar, br), minus(ai, bi)))
        odd.append(times((minus(ar, br), plus(ai, bi)), np.exp(2j * np.pi * k / n)))
    out = [None] * n
    out[0::2] = inverse_real(even)
    out[1::2] = inverse_real(odd)
    return out


def tables(circle):
    first = circle // LANES
    half = first // 2 + 1
    b = np.arange(LANES)
    angle = 2.0 * np.pi / LANES * (np.outer(b, b) % LANES)
    c, s = np.cos(angle), np.sin(angle)
    ahead = np.block([[c, -s], [s, c]])
    back = np.block([[c, s], [-s, c]]) / circle
    turn = 2.0 * np.pi / circle * np.outer(np.arange(half), b)
    padded = -(-half // TILE) * TILE
    twist = np.zeros((2, padded, LANES))
    twist[0, :half], twist[1, :half] = np.cos(turn), np.sin(turn)
    return [x.astype(np.float32) for x in (ahead, back, twist)]


class Plan:
    def __init__(self, lat_count, lon_count, row_count, polar):
        self.chunk = TILE * lon_count
        self.workers = lat_count // 2
        bands = -(-polar // row_count)
        self.chunks = [
            -(-min(row_count, polar - b * row_count) // self.chunk) for b in range(bands)
        ]
        pairs = {}
        for b in range(bands):
            for f in range(6):
                if bands == 2 and self.workers >= 4:
                    pairs[b, f] = f % 3 if b == 0 else (3 if f < 5 else 1)
                else:
                    pairs[b, f] = (6 * b + f) % self.workers
        self.slots = [[] for _ in range(self.workers)]
        self.where = {}
        for c in range(max(self.chunks)):
            for b in range(bands):
                for f in range(6):
                    if c < self.chunks[b]:
                        w = pairs[b, f]
                        self.where[b, c, f] = (w, len(self.slots[w]))
                        self.slots[w].append((b, c, f))
        self.most = max(len(x) for x in self.slots)
        self.partners = [set() for _ in range(self.workers)]
        for (b, _, _), (w, _) in self.where.items():
            self.partners[b].add(w)
            self.partners[w].add(b)


def filter_kernel(
    plan, tend, keep, ahead, behind, twist, back, taken, made, spec, sent, got, returned, home
):
    lat_count, lon_count = lax.axis_size("lat"), lax.axis_size("lon")
    lat, lon = lax.axis_index("lat"), lax.axis_index("lon")
    row_count, col_count = tend.shape[1:]
    circle = col_count * lon_count
    first = circle // LANES
    half = first // 2 + 1
    north = lat >= lat_count // 2
    band = jnp.where(north, lat_count - 1 - lat, lat)

    def real_band(b):
        return jnp.where(north, lat_count - 1 - b, b)

    def chunk_row(b, c):
        base = jnp.where(north, row_count - plan.chunks[b] * plan.chunk, 0)
        return base + c * plan.chunk

    barrier = pltpu.get_barrier_semaphore()
    for b in range(plan.workers):
        count = 0
        others = sorted(plan.partners[b])
        if not others:
            continue

        @pl.when(band == b)
        def _():
            count = 0
            for other in others:
                for hop in range(lon_count):
                    if other == b and hop == 0:
                        continue
                    pl.semaphore_signal(
                        barrier,
                        inc=1,
                        device_id=(real_band(other), lax.rem(lon + hop, lon_count)),
                        device_id_type=MESH,
                    )
                    count += 1
            pl.semaphore_wait(barrier, count)

    mine = pl.ds(pl.multiple_of(lon * col_count, LANES), col_count)
    for b in range(len(plan.chunks)):

        @pl.when(band == b)
        def _():
            for c in range(plan.chunks[b]):
                for f in range(6):
                    worker, slot = plan.where[b, c, f]
                    for hop in list(range(1, lon_count)) + [0]:
                        peer = lax.rem(lon + hop, lon_count)
                        start = pl.multiple_of(chunk_row(b, c) + peer * TILE, TILE)
                        source = tend.at[f, pl.ds(start, TILE), :]
                        target = taken.at[slot, :, mine]
                        if hop == 0 and worker == b:
                            pltpu.make_async_copy(source, target, got.at[slot]).start()
                        else:
                            pltpu.make_async_remote_copy(
                                src_ref=source,
                                dst_ref=target,
                                send_sem=sent.at[c * 6 + f],
                                recv_sem=got.at[slot],
                                device_id=(real_band(worker), peer),
                                device_id_type=MESH,
                            ).start()

    slot_count = jnp.int32(0)
    for w in range(plan.workers):
        slot_count = jnp.where(band == w, len(plan.slots[w]), slot_count)

    def one(slot, _):
        pltpu.make_async_copy(taken.at[slot], taken.at[slot], got.at[slot]).wait()
        parts = forward_real(
            [taken[slot, :, a * LANES : (a + 1) * LANES] for a in range(first)]
        )
        for k in range(half):
            re, im = parts[k]
            c, s = twist[0, k : k + 1, :], twist[1, k : k + 1, :]
            if im is None:
                tr, ti = re * c, -(re * s)
            else:
                tr, ti = re * c + im * s, im * c - re * s
            spec[k * TILE : (k + 1) * TILE, 0:LANES] = tr
            spec[k * TILE : (k + 1) * TILE, LANES : 2 * LANES] = ti
        freq = jnp.dot(
            spec[...],
            ahead[...],
            precision=lax.Precision.HIGHEST,
            preferred_element_type=jnp.float32,
        )
        number = lax.broadcasted_iota(jnp.int32, (half, TILE, 2 * LANES), 0) + first * (
            lax.broadcasted_iota(jnp.int32, (half, TILE, 2 * LANES), 2) % LANES
        )
        folded = jnp.minimum(number, circle - number)
        kept = jnp.tile(keep[slot], (1, 2))
        freq = freq.reshape(half, TILE, 2 * LANES)
        freq = jnp.where(folded < kept[None], freq, 0.0).reshape(half * TILE, 2 * LANES)
        spec[...] = jnp.dot(
            freq,
            behind[...],
            precision=lax.Precision.HIGHEST,
            preferred_element_type=jnp.float32,
        )
        turned = []
        for k in range(half):
            re = spec[k * TILE : (k + 1) * TILE, 0:LANES]
            im = spec[k * TILE : (k + 1) * TILE, LANES : 2 * LANES]
            c, s = twist[0, k : k + 1, :], twist[1, k : k + 1, :]
            turned.append((re * c - im * s, re * s + im * c))
        signal = inverse_real(turned)
        for a in range(first):
            made[slot, :, a * LANES : (a + 1) * LANES] = signal[a]
        for w in range(plan.workers):
            for index, (b, c, f) in enumerate(plan.slots[w]):

                @pl.when((band == w) & (slot == index))
                def _():
                    for hop in list(range(1, lon_count)) + [0]:
                        peer = lax.rem(lon + hop, lon_count)
                        cols = pl.ds(pl.multiple_of(peer * col_count, LANES), col_count)
                        start = pl.multiple_of(chunk_row(b, c) + lon * TILE, TILE)
                        source = made.at[index, :, cols]
                        target = back.at[f, pl.ds(start, TILE), :]
                        if hop == 0 and w == b:
                            pltpu.make_async_copy(source, target, home.at[f]).start()
                        else:
                            pltpu.make_async_remote_copy(
                                src_ref=source,
                                dst_ref=target,
                                send_sem=returned.at[index],
                                recv_sem=home.at[f],
                                device_id=(real_band(b), peer),
                                device_id_type=MESH,
                            ).start()

        return 0

    lax.fori_loop(0, slot_count, one, 0)

    for b in range(len(plan.chunks)):

        @pl.when(band == b)
        def _():
            for c in range(plan.chunks[b]):
                for f in range(6):
                    worker, _ = plan.where[b, c, f]
                    count = lon_count - 1 if worker == b else lon_count
                    span = tend.at[f, 0 : count * TILE, :]
                    pltpu.make_async_copy(span, span, sent.at[c * 6 + f]).wait()
            for f in range(6):
                span = back.at[f, 0 : plan.chunks[b] * plan.chunk, :]
                pltpu.make_async_copy(span, span, home.at[f]).wait()

    for w in range(plan.workers):
        if not plan.slots[w]:
            continue

        @pl.when(band == w)
        def _():
            for index, (b, _, _) in enumerate(plan.slots[w]):
                count = lon_count - 1 if w == b else lon_count
                span = made.at[index, :, 0 : count * col_count]
                pltpu.make_async_copy(span, span, returned.at[index]).wait()


def cap_filter(plan, tend, keep, ahead, behind, twist):
    row_count, col_count = tend.shape[1:]
    circle = col_count * lax.axis_size("lon")
    half = circle // LANES // 2 + 1
    vmem = pl.BlockSpec(memory_space=pltpu.VMEM)
    anywhere = pl.BlockSpec(memory_space=pl.ANY)
    return pl.pallas_call(
        functools.partial(filter_kernel, plan),
        out_shape=jax.ShapeDtypeStruct(tend.shape, jnp.float32),
        in_specs=[anywhere, vmem, vmem, vmem, vmem],
        out_specs=anywhere,
        scratch_shapes=[
            pltpu.VMEM((plan.most, TILE, circle), jnp.float32),
            pltpu.VMEM((plan.most, TILE, circle), jnp.float32),
            pltpu.VMEM((half * TILE, 2 * LANES), jnp.float32),
            pltpu.SemaphoreType.DMA((6 * max(plan.chunks),)),
            pltpu.SemaphoreType.DMA((plan.most,)),
            pltpu.SemaphoreType.DMA((plan.most,)),
            pltpu.SemaphoreType.DMA((6,)),
        ],
        compiler_params=pltpu.CompilerParams(
            collective_id=0, has_side_effects=True, vmem_limit_bytes=LIMIT
        ),
        name="cap_filter",
    )(tend, keep, ahead, behind, twist)


def kept_counts(plan, cutoffs, row_count, total_rows, polar):
    lat_count = lax.axis_size("lat")
    starts = np.zeros((lat_count, plan.most), np.int32)
    for lat in range(lat_count):
        north = lat >= lat_count // 2
        band = lat_count - 1 - lat if north else lat
        for slot, (b, c, _) in enumerate(plan.slots[band]):
            base = row_count - plan.chunks[b] * plan.chunk if north else 0
            real = lat_count - 1 - b if north else b
            starts[lat, slot] = real * row_count + base + c * plan.chunk
    start = lax.dynamic_index_in_dim(jnp.asarray(starts), lax.axis_index("lat"), keepdims=False)
    rows = (
        start[:, None]
        + lax.axis_index("lon") * TILE
        + jnp.arange(TILE, dtype=jnp.int32)[None, :]
    ).reshape(-1)
    position = jnp.where(rows < polar, rows, rows - (total_rows - 2 * polar))
    ids = jnp.arange(2 * polar, dtype=jnp.int32)
    counts = jnp.sum(
        jnp.where(position[:, None] == ids[None, :], cutoffs[None, :], 0), axis=1, dtype=jnp.int32
    )
    return jnp.broadcast_to(counts.reshape(plan.most, TILE, 1), (plan.most, TILE, LANES))


def geometry(row_start, row_count, total_rows):
    ids = row_start - TILE + jnp.arange(row_count + 2 * TILE, dtype=jnp.int32)
    spacing = math.pi / total_rows
    centre = -0.5 * math.pi + (ids.astype(jnp.float32) + 0.5) * spacing
    face = -0.5 * math.pi + (ids.astype(jnp.float32) + 1.0) * spacing
    live = jnp.where((ids >= 0) & (ids < total_rows - 1), 1.0, 0.0).astype(jnp.float32)
    centre_cos = jnp.cos(centre)
    face_cos = jnp.cos(face) * live
    face_inverse = live / (face_cos + (1.0 - live))
    coefs = jnp.stack(
        [centre_cos, 1.0 / centre_cos, face_cos, CORIOLIS * jnp.sin(face), face_inverse, live]
    )
    return jnp.broadcast_to(coefs[:, :, None], coefs.shape + (LANES,))


def rims(fields):
    lat_count, lon_count = lax.axis_size("lat"), lax.axis_size("lon")
    up = [(i, i + 1) for i in range(lat_count - 1)]
    down = [(i + 1, i) for i in range(lat_count - 1)]
    south = lax.ppermute(fields[:, -1:, :], "lat", up)
    north = lax.ppermute(fields[:, :1, :], "lat", down)
    right = [(i, (i + 1) % lon_count) for i in range(lon_count)]
    left = [((i + 1) % lon_count, i) for i in range(lon_count)]
    last = jnp.concatenate([south[:, :, -1:], fields[:, :, -1:], north[:, :, -1:]], axis=1)
    head = jnp.concatenate([south[:, :, :1], fields[:, :, :1], north[:, :, :1]], axis=1)
    west = lax.ppermute(last[:, :, 0], "lon", right)
    east = lax.ppermute(head[:, :, 0], "lon", left)
    rows = jnp.concatenate(
        [
            jnp.pad(south, ((0, 0), (TILE - 1, 0), (0, 0))),
            jnp.pad(north, ((0, 0), (0, TILE - 1), (0, 0))),
        ],
        axis=1,
    )
    edge = ((0, 0), (TILE - 1, TILE - 1))
    west, east = jnp.pad(west, edge), jnp.pad(east, edge)
    lane = jnp.arange(2 * LANES, dtype=jnp.int32)
    cols = jnp.where(lane == LANES - 1, west[:, :, None], jnp.where(lane == LANES, east[:, :, None], 0.0))
    return rows, cols


def body(thickness, winds, terrain, cutoffs):
    row_count = thickness.shape[1]
    col_count = thickness.shape[2]
    lat_count, lon_count = lax.axis_size("lat"), lax.axis_size("lon")
    total_rows = row_count * lat_count
    circle = col_count * lon_count
    polar = (total_rows + 2) // 6
    plan = Plan(lat_count, lon_count, row_count, polar)
    row_start = lax.axis_index("lat") * row_count
    global_rows = row_start + jnp.arange(row_count, dtype=jnp.int32)
    live = jnp.where(global_rows < total_rows - 1, 1.0, 0.0).astype(jnp.float32)
    capped = ((global_rows < polar) | (global_rows >= total_rows - polar))[None, :, None]
    coefs = geometry(row_start, row_count, total_rows)
    keep = kept_counts(plan, cutoffs, row_count, total_rows, polar)
    ahead, behind, twist = [jnp.asarray(x) for x in tables(circle)]
    current = jnp.concatenate([thickness, winds[0], winds[1] * live[None, :, None]], axis=0)
    step_size = 0.1 * min(1.0, circle / (2.0 * total_rows))
    anchor = current
    ground_rows, ground_cols = rims(terrain[None])
    for fraction in (1.0 / 3.0, 0.5, 1.0):
        rows, cols = rims(current)
        rows = jnp.concatenate([rows, ground_rows], axis=0)
        cols = jnp.concatenate([cols, ground_cols], axis=0)
        tendency = stencil(current, rows, cols, terrain, coefs)
        filtered = cap_filter(plan, tendency, keep, ahead, behind, twist)
        current = anchor + fraction * step_size * jnp.where(capped, filtered, tendency)
    return (current[0:2], current[2:6].reshape(2, 2, row_count, col_count))


def solution(mesh):
    in_specs = (P(None, "lat", "lon"), P(None, None, "lat", "lon"), P("lat", "lon"), P())
    out_specs = (P(None, "lat", "lon"), P(None, None, "lat", "lon"))
    return jax.shard_map(body, mesh=mesh, in_specs=in_specs, out_specs=out_specs, check_vma=False)
```

time: 1550 us -> 441 us (0.28)
  blocking collectives: 710 us -> 0 us
  Pallas kernels: 0 us -> 350 us
  local copies, waits for them, and re-layouts: 230 us -> 20.4 us
  other arithmetic: 228 us -> 31.9 us
  waiting for transfers between devices: 192 us -> 16.7 us
  matrix products: 163 us -> 0 us
    all_to_all x5 -> x0, blocking collectives: 710 us -> none  [the longest x3 428 us: cap_filter(): lax.all_to_all(filtered.reshape(channels, groups, device_count, col_count...]
    pallas_call x0 -> x6, Pallas kernels: none -> 350 us  [the longest x3 286 us: cap_filter(): pl.pallas_call(functools.partial(filter_kernel, plan), out_shape=jax.Shap...]
    dot_general x72 -> x0, matrix products: 163 us -> none  [the longest x6 22.3 us: spectral_filter(): part_imag = -jnp.einsum('mab,ak->mkb', grid, sin_first, precision=highest)]
    all_to_all x1 -> x0, waiting for transfers between devices: 139 us -> none  [cap_filter(): lax.all_to_all(outgoing, ('lat', 'lon'), split_axis=2, concat_axis=2, til...]
    reshape x20 -> x0, local copies, waits for them, and re-layouts: 101 us -> none  [the longest x6 44 us: cap_filter(): filtered.reshape(channels, groups, device_count, col_count)]
    concatenate x14 -> x13, other arithmetic: 76.1 us -> 7.56 us  [the longest x3 3.22 us: body(): rows = jnp.concatenate([rows, ground_rows], axis=0)]
    mul x18 -> x1, other arithmetic: 53.6 us -> 0.08 us  [geometry(): face_cos = jnp.cos(face) * live]
    div x3 -> x1, other arithmetic: 36.5 us -> 0.08 us  [geometry(): 1.0 / centre_cos]
  transfers between devices with their start and end apart: 13 -> 16, of which waited for: 13 -> 7; matrix products, arithmetic and copies ran while one was open for 0% -> 4% of each run, Pallas kernels for 0% -> 0%
where the time goes in v1:
time: 441 us; the launch traced here: 440 us
  Pallas kernels  350 us (79%)
  other arithmetic  31.9 us (7%)
  local copies, waits for them, and re-layouts  20.4 us (5%)
  starting transfers between devices  19.8 us (4%)
  waiting for transfers between devices  16.7 us (4%)
    pallas_call x3, Pallas kernels, cap_filter(): pl.pallas_call(functools.partial(filter_kernel, plan), out_shape=jax.Shap...  286 us
    pallas_call x3, Pallas kernels, stencil(): pl.pallas_call(stencil_kernel, out_shape=jax.ShapeDtypeStruct(state.shape...  64.2 us
    add x3, other arithmetic, body(): anchor + fraction * step_size * jnp.where(capped, filtered, tendency)  16.9 us
    ppermute x4, starting transfers between devices, rims(): south = lax.ppermute(fields[:, -1:, :], 'lat', up)  12 us
    ppermute x4, waiting for transfers between devices, rims(): north = lax.ppermute(fields[:, :1, :], 'lat', down)  9.21 us
  transfers between devices with their start and end apart: 16, of which 7 were waited for; matrix products, arithmetic and copies ran while one was open for 4% of the time, Pallas kernels for 0%

profile of v1, /device:TPU:0, one launch (start us, length us, event | category | flops | bytes accessed | tf_op | source)
XLA Modules:
  0.0 440.1 jit_solution(8340072728718534568)
XLA Ops:
  0.6 1.0 fusion.15
  1.7 4.8 %collective-permute-start.2 = (f32[1,1,2048]{2,1,0:T(1,128)S(1)}, f32[1,1,2048]{2,1,0:T(1,128)S(1)}, u32[]{:S(2)}, u32[]{:S(2)}) collective-permute-start(f32[1,1,2048]{2,1,0:T(1,128)S(1)} %get-tuple-element.16), channel_id=1, source_target_pairs={{0,4},{4,8},{8,12},{12,16},{16,20},{20,24},{24,28},{1,5},{5,9},{9,... | collective-permute-start | bytes 24584 | tf_op jit(solution)/shard_map/ppermute | solution.py:477
  6.5 1.3 collective-permute-start.3
  7.8 1.7 slice_bitcast_fusion
  9.6 2.7 bitcast_multiply_fusion
  12.3 0.7 pad_maximum_fusion.state_ref
  13.0 0.7 copy-done.4
  13.8 2.6 copy-done.6
  16.4 4.5 %collective-permute-start = (f32[6,1,2048]{2,1,0:T(1,128)S(1)}, f32[6,1,2048]{2,1,0:T(1,128)S(1)}, u32[]{:S(2)}, u32[]{:S(2)}) collective-permute-start(f32[6,1,2048]{2,1,0:T(1,128)S(1)} %get-tuple-element.12), channel_id=1, source_target_pairs={{0,4},{4,8},{8,12},{12,16},{16,20},{20,24},{24,28},{1,5},{5,9},{9,... | collective-permute-start | bytes 147464 | tf_op jit(solution)/shard_map/ppermute | solution.py:477
  20.9 1.3 collective-permute-start.1
  22.5 1.0 fusion.14
  23.4 1.3 fusion.12
  24.7 0.7 add_bitcast_fusion
  26.9 0.6 fusion.17
  27.6 1.4 maximum_bitcast_fusion.1
  29.1 1.2 maximum_bitcast_fusion
  30.8 2.5 collective-permute-done.6
  34.4 1.1 fusion.4.rows_ref
  35.6 1.5 collective-permute-done.4
  37.4 1.1 pad_maximum_fusion.3.cols_ref
  38.5 1.0 broadcast_in_dim.176.coef_ref
  39.4 21.4 %stencil.3.tend = f32[6,128,2048]{2,1,0:T(8,128)} custom-call(f32[6,128,2048]{2,1,0:T(8,128)} %copy-done.6, f32[7,16,2048]{2,1,0:T(8,128)} %fusion.4.rows_ref, f32[7,144,256]{2,1,0:T(8,128)} %pad_maximum_fusion.3.cols_ref, f32[128,2048]{1,0:T(8,128)} %ground_ref.5, f32[6,144,128]{2,1,0:T(8,128)} %broadcast_in_dim.176.coef_ref), custom_call_target="tpu_custom_call" | custom-call | tf_op jit(solution)/shard_map/stencil/pallas_call | solution.py:118
  60.8 0.7 broadcast_in_dim.180.keep
  61.5 97.9 %cap_filter.3 = f32[6,128,2048]{2,1,0:T(8,128)} custom-call(f32[6,128,2048]{2,1,0:T(8,128)} %stencil.3.tend, s32[10,8,128]{2,1,0:T(8,128)} %broadcast_in_dim.180.keep, f32[256,256]{1,0:T(8,128)} %constant.63.clone.ahead, f32[256,256]{1,0:T(8,128)} %constant.64.clone.behind, f32[2,40,128]{2,1,0:T(8,128)} %constant.65.clone.twist), custom_call_target="tpu_custom_call" | custom-call | tf_op jit(solution)/shard_map/cap_filter/pallas_call | solution.py:413
  159.5 5.6 %multiply_add_fusion.2.state_ref = f32[6,128,2048]{2,1,0:T(8,128)S(1)} fusion(f32[6,128,2048]{2,1,0:T(8,128)} %cap_filter.3, f32[6,128,2048]{2,1,0:T(8,128)S(1)} %copy-done.1, pred[128]{0:T(512)(128)(4,1)S(1)} %compare_or_fusion, f32[2,128,2048]{2,1,0:T(8,128)} %copy-done.4, f32[2,128,2048]{2,1,0:T(8,128)} %copy-done.3, f32[2,128,2048]{2,1,0:T(8,128)} %param.8), kind=kLoop, calls=%fused_computation.3 | loop fusion | flops 7864320 | bytes 25165952 | tf_op jit(solution)/shard_map/add | solution.py:524
  165.2 1.3 collective-permute-start.8
  166.5 1.3 copy-done.8
  168.0 1.3 collective-permute-start.9
  169.7 4.6 %collective-permute-done.9 = f32[6,1,2048]{2,1,0:T(1,128)S(1)} collective-permute-done((f32[6,1,2048]{2,1,0:T(1,128)S(1)}, f32[6,1,2048]{2,1,0:T(1,128)S(1)}, u32[]{:S(2)}, u32[]{:S(2)}) %collective-permute-start.9) | collective-permute-done | bytes 49184 | tf_op jit(solution)/shard_map/ppermute | solution.py:478
  174.5 1.0 collective-permute-start.11
  175.5 1.1 fusion.1.rows_ref
  177.0 1.6 collective-permute-done.10
  179.0 1.1 pad_maximum_fusion.2.cols_ref
  180.0 21.4 %stencil.4.tend = f32[6,128,2048]{2,1,0:T(8,128)} custom-call(f32[6,128,2048]{2,1,0:T(8,128)} %copy-done.8, f32[7,16,2048]{2,1,0:T(8,128)} %fusion.1.rows_ref, f32[7,144,256]{2,1,0:T(8,128)} %pad_maximum_fusion.2.cols_ref, f32[128,2048]{1,0:T(8,128)} %ground_ref.5, f32[6,144,128]{2,1,0:T(8,128)} %broadcast_in_dim.176.coef_ref), custom_call_target="tpu_custom_call" | custom-call | tf_op jit(solution)/shard_map/stencil/pallas_call | solution.py:118
  201.5 94.0 %cap_filter.4 = f32[6,128,2048]{2,1,0:T(8,128)} custom-call(f32[6,128,2048]{2,1,0:T(8,128)} %stencil.4.tend, s32[10,8,128]{2,1,0:T(8,128)} %broadcast_in_dim.180.keep, f32[256,256]{1,0:T(8,128)} %constant.63.clone.ahead, f32[256,256]{1,0:T(8,128)} %constant.64.clone.behind, f32[2,40,128]{2,1,0:T(8,128)} %constant.65.clone.twist), custom_call_target="tpu_custom_call" | custom-call | tf_op jit(solution)/shard_map/cap_filter/pallas_call | solution.py:413
  295.5 5.6 %multiply_add_fusion.1.state_ref = f32[6,128,2048]{2,1,0:T(8,128)S(1)} fusion(f32[6,128,2048]{2,1,0:T(8,128)} %cap_filter.4, f32[6,128,2048]{2,1,0:T(8,128)S(1)} %copy-done.2, pred[128]{0:T(512)(128)(4,1)S(1)} %compare_or_fusion, f32[2,128,2048]{2,1,0:T(8,128)} %copy-done.4, f32[2,128,2048]{2,1,0:T(8,128)} %copy-done.3, f32[2,128,2048]{2,1,0:T(8,128)} %param.8), kind=kLoop, calls=%fused_computation.2 | loop fusion | flops 7864320 | bytes 25165952 | tf_op jit(solution)/shard_map/add | solution.py:524
  301.2 1.3 collective-permute-start.12
  302.5 1.3 copy-done.7
  304.0 1.3 collective-permute-start.13
  305.7 4.6 %collective-permute-done.13 = f32[6,1,2048]{2,1,0:T(1,128)S(1)} collective-permute-done((f32[6,1,2048]{2,1,0:T(1,128)S(1)}, f32[6,1,2048]{2,1,0:T(1,128)S(1)}, u32[]{:S(2)}, u32[]{:S(2)}) %collective-permute-start.13) | collective-permute-done | bytes 49184 | tf_op jit(solution)/shard_map/ppermute | solution.py:478
  311.1 1.1 fusion.rows_ref
  312.3 1.6 collective-permute-done.14
  314.2 1.1 pad_maximum_fusion.1.cols_ref
  315.3 21.4 %stencil.5.tend = f32[6,128,2048]{2,1,0:T(8,128)} custom-call(f32[6,128,2048]{2,1,0:T(8,128)} %copy-done.7, f32[7,16,2048]{2,1,0:T(8,128)} %fusion.rows_ref, f32[7,144,256]{2,1,0:T(8,128)} %pad_maximum_fusion.1.cols_ref, f32[128,2048]{1,0:T(8,128)} %ground_ref.5, f32[6,144,128]{2,1,0:T(8,128)} %broadcast_in_dim.176.coef_ref), custom_call_target="tpu_custom_call" | custom-call | tf_op jit(solution)/shard_map/stencil/pallas_call | solution.py:118
  336.7 94.0 %cap_filter.5 = f32[6,128,2048]{2,1,0:T(8,128)} custom-call(f32[6,128,2048]{2,1,0:T(8,128)} %stencil.5.tend, s32[10,8,128]{2,1,0:T(8,128)} %broadcast_in_dim.180.keep, f32[256,256]{1,0:T(8,128)} %constant.63.clone.ahead, f32[256,256]{1,0:T(8,128)} %constant.64.clone.behind, f32[2,40,128]{2,1,0:T(8,128)} %constant.65.clone.twist), custom_call_target="tpu_custom_call" | custom-call | tf_op jit(solution)/shard_map/cap_filter/pallas_call | solution.py:413
  430.7 5.6 %multiply_add_fusion = f32[6,128,2048]{2,1,0:T(8,128)S(1)} fusion(f32[6,128,2048]{2,1,0:T(8,128)} %cap_filter.5, f32[6,128,2048]{2,1,0:T(8,128)S(1)} %copy-done, pred[128]{0:T(512)(128)(4,1)S(1)} %compare_or_fusion, f32[2,128,2048]{2,1,0:T(8,128)} %copy-done.4, f32[2,128,2048]{2,1,0:T(8,128)} %copy-done.3, f32[2,128,2048]{2,1,0:T(8,128)} %param.8), kind=kLoop, calls=%fused_computation.1 | loop fusion | flops 7864320 | bytes 25165952 | tf_op jit(solution)/shard_map/add | solution.py:524
  436.4 1.5 slice.176
  437.8 2.3 slice.177
  (89 shorter events, 7.5 us)
Async XLA Ops:
  0.6 11.7 %copy-start.5 = (f32[2,128,2048]{2,1,0:T(8,128)S(1)}, f32[2,128,2048]{2,1,0:T(8,128)}, u32[]{:S(2)}) copy-start(f32[2,128,2048]{2,1,0:T(8,128)} %param.8) | copy-start | bytes 6291460
  1.7 24.7 %collective-permute-start.2 = (f32[1,1,2048]{2,1,0:T(1,128)S(1)}, f32[1,1,2048]{2,1,0:T(1,128)S(1)}, u32[]{:S(2)}, u32[]{:S(2)}) collective-permute-start(f32[1,1,2048]{2,1,0:T(1,128)S(1)} %get-tuple-element.16), channel_id=1, source_target_pairs={{0,4},{4,8},{8,12},{12,16},{16,20},{20,24},{24,28},{1,5},{5,9},{9,... | collective-permute-start | bytes 24584 | tf_op jit(solution)/shard_map/ppermute | solution.py:477
  6.5 20.4 %collective-permute-start.3 = (f32[1,1,2048]{2,1,0:T(1,128)S(1)}, f32[1,1,2048]{2,1,0:T(1,128)S(1)}, u32[]{:S(2)}, u32[]{:S(2)}) collective-permute-start(f32[1,1,2048]{2,1,0:T(1,128)S(1)} %get-tuple-element.17), channel_id=1, source_target_pairs={{4,0},{8,4},{12,8},{16,12},{20,16},{24,20},{28,24},{5,1},{9,5},{13... | collective-permute-start | bytes 24584 | tf_op jit(solution)/shard_map/ppermute | solution.py:478
  9.6 3.4 copy-start.3
  12.3 1.4 copy-start.4
  12.3 13.3 %copy-start.9 = (s32[342]{0:T(512)S(1)}, s32[342]{0:T(512)}, u32[]{:S(2)}) copy-start(s32[342]{0:T(512)} %param.11) | copy-start | bytes 4108
  13.7 2.7 copy-start.6
  16.4 17.1 %collective-permute-start = (f32[6,1,2048]{2,1,0:T(1,128)S(1)}, f32[6,1,2048]{2,1,0:T(1,128)S(1)}, u32[]{:S(2)}, u32[]{:S(2)}) collective-permute-start(f32[6,1,2048]{2,1,0:T(1,128)S(1)} %get-tuple-element.12), channel_id=1, source_target_pairs={{0,4},{4,8},{8,12},{12,16},{16,20},{20,24},{24,28},{1,5},{5,9},{9,... | collective-permute-start | bytes 147464 | tf_op jit(solution)/shard_map/ppermute | solution.py:477
  20.9 12.6 %collective-permute-start.1 = (f32[6,1,2048]{2,1,0:T(1,128)S(1)}, f32[6,1,2048]{2,1,0:T(1,128)S(1)}, u32[]{:S(2)}, u32[]{:S(2)}) collective-permute-start(f32[6,1,2048]{2,1,0:T(1,128)S(1)} %get-tuple-element.13), channel_id=1, source_target_pairs={{4,0},{8,4},{12,8},{16,12},{20,16},{24,20},{28,24},{5,1},{9,5},{13... | collective-permute-start | bytes 147464 | tf_op jit(solution)/shard_map/ppermute | solution.py:478
  28.9 1.8 collective-permute-start.7
  30.3 3.0 collective-permute-start.6
  33.9 1.6 collective-permute-start.5
  33.9 3.1 collective-permute-start.4
  61.5 97.9 %copy-start.1 = (f32[6,128,2048]{2,1,0:T(8,128)S(1)}, f32[6,128,2048]{2,1,0:T(8,128)}, u32[]{:S(2)}) copy-start(f32[6,128,2048]{2,1,0:T(8,128)} %stencil.3.tend) | copy-start | bytes 18874372
  165.1 2.6 copy-start.8
  165.2 4.4 collective-permute-start.8
  168.0 6.3 %collective-permute-start.9 = (f32[6,1,2048]{2,1,0:T(1,128)S(1)}, f32[6,1,2048]{2,1,0:T(1,128)S(1)}, u32[]{:S(2)}, u32[]{:S(2)}) collective-permute-start(f32[6,1,2048]{2,1,0:T(1,128)S(1)} %get-tuple-element.9), channel_id=1, source_target_pairs={{4,0},{8,4},{12,8},{16,12},{20,16},{24,20},{28,24},{5,1},{9,5},{13... | collective-permute-start | bytes 147464 | tf_op jit(solution)/shard_map/ppermute | solution.py:478
  174.5 2.4 collective-permute-start.11
  175.5 3.1 collective-permute-start.10
  201.5 94.0 %copy-start.2 = (f32[6,128,2048]{2,1,0:T(8,128)S(1)}, f32[6,128,2048]{2,1,0:T(8,128)}, u32[]{:S(2)}) copy-start(f32[6,128,2048]{2,1,0:T(8,128)} %stencil.4.tend) | copy-start | bytes 18874372
  301.1 2.6 copy-start.7
  301.2 4.4 collective-permute-start.12
  304.0 6.3 %collective-permute-start.13 = (f32[6,1,2048]{2,1,0:T(1,128)S(1)}, f32[6,1,2048]{2,1,0:T(1,128)S(1)}, u32[]{:S(2)}, u32[]{:S(2)}) collective-permute-start(f32[6,1,2048]{2,1,0:T(1,128)S(1)} %get-tuple-element.5), channel_id=1, source_target_pairs={{4,0},{8,4},{12,8},{16,12},{20,16},{24,20},{28,24},{5,1},{9,5},{13... | collective-permute-start | bytes 147464 | tf_op jit(solution)/shard_map/ppermute | solution.py:478
  310.6 1.6 collective-permute-start.15
  310.8 3.1 collective-permute-start.14
  336.7 94.0 %copy-start = (f32[6,128,2048]{2,1,0:T(8,128)S(1)}, f32[6,128,2048]{2,1,0:T(8,128)}, u32[]{:S(2)}) copy-start(f32[6,128,2048]{2,1,0:T(8,128)} %stencil.5.tend) | copy-start | bytes 18874372
